TPU v7x, 256 devices: a whole 4x4x8 slice. The times are simulated.
256 devices in a mesh: gx: 8 (over x, core), gyz: 8 (over y, z_lo), band: 4 (over z_hi).
Axes of the slice: x: 4, y: 4, z: 8 (z_hi: 4, z_lo: 2; z = z_hi * 2 + z_lo), core: 2. Of those that a mesh axis runs over, the one named last changes fastest.
Arguments:
- orbitals: float32 [256, 32, 64, 128], P('band', 'gx', 'gyz'), may hold values from -6 to 6
- v_local: float32 [32, 64, 128], P('gx', 'gyz'), may hold values from 0 to 2
- features: bfloat16 [11, 32, 64, 128], P(None, 'gx', 'gyz'), may hold values from -6 to 6
- w_first: bfloat16 [256, 11], replicated, may hold values from -1.75 to 1.75
- w_hidden: bfloat16 [1, 256, 256], replicated, may hold values from -0.375 to 0.375
- w_last: bfloat16 [256], replicated, may hold values from -0.375 to 0.375
- rotation: float32 [256, 256], replicated, may hold values from -0.375 to 0.375
- assignment: int32 [256], replicated, may hold values from 0 to 255, each once
- degrees: int32 [256], P('band'), may hold values from 4 to 8, as said below
Outputs:
- gram: float32 [256, 256], P('band')
- rotated: float32 [256, 32, 64, 128], P('band', 'gx', 'gyz')
Inputs may be any that keep to these rules, and one draw needn't show every extreme that they name: `degrees`: a filter degree of each slot; some slot has 8 and some has 4. `assignment`: each orbital is held in exactly one slot.
All inputs are finite; a program needn't handle non-finite values.
Results may differ from a plain program's by a relative error of at most 0.0043.
Values may be sent and summed in bfloat16 or wider, within the bound.
No kernel may reach another device: no remote copies, remote signals or barrier semaphores. Data moves between devices by JAX's collectives and lax.ppermute only.
A program may use at most 64 MiB of HBM per device.

v0:
```python
import jax
import jax.numpy as jnp
from jax import lax
from jax.sharding import PartitionSpec as P

DEG = 8
LOWER_EDGE = 2.0
CUT_EDGE = 3.0
UPPER_EDGE = 9.5


def with_halo(block, sides, width):
    for axis, dim in sides:
        count = lax.axis_size(axis)
        forward = [(i, i + 1) for i in range(count - 1)]
        backward = [(target, source) for source, target in forward]
        low = lax.ppermute(
            lax.slice_in_dim(block, block.shape[dim] - width, None, axis=dim), axis, forward
        )
        high = lax.ppermute(lax.slice_in_dim(block, 0, width, axis=dim), axis, backward)
        block = jnp.concatenate([low, block, high], axis=dim)
    return block


def coefficients(count):
    half_width = (UPPER_EDGE - CUT_EDGE) / 2.0
    centre = (UPPER_EDGE + CUT_EDGE) / 2.0
    first = half_width / (LOWER_EDGE - centre)
    factors = [(first / half_width, 0.0)]
    sigma = first
    for rounds in range(1, count):
        updated = 1.0 / (2.0 / first - sigma)
        factors.append((2.0 * updated / half_width, sigma * updated))
        sigma = updated
    return (factors, centre)


def hamiltonian(field, potential):
    padded = with_halo(field, (("gx", 1), ("gyz", 2)), 1)
    padded = jnp.pad(padded, ((0, 0), (0, 0), (0, 0), (1, 1)))
    beside_all = padded[:, 2:, 1:-1, 1:-1] + padded[:, :-2, 1:-1, 1:-1]
    beside_all = beside_all + padded[:, 1:-1, 2:, 1:-1] + padded[:, 1:-1, :-2, 1:-1]
    beside_all = beside_all + padded[:, 1:-1, 1:-1, 2:] + padded[:, 1:-1, 1:-1, :-2]
    return 0.5 * (6.0 * field - beside_all) + potential * field


def network(cell_features, w_first, w_hidden, w_last):
    feature_count = cell_features.shape[0]
    flattened = cell_features.reshape(feature_count, -1)
    hidden = jax.nn.silu(jnp.dot(w_first, flattened, preferred_element_type=jnp.float32)).astype(
        jnp.bfloat16
    )
    hidden = jax.nn.silu(jnp.dot(w_hidden[0], hidden, preferred_element_type=jnp.float32)).astype(
        jnp.bfloat16
    )
    values = jnp.tanh(jnp.dot(w_last[None, :], hidden, preferred_element_type=jnp.float32)[0])
    return values.reshape(cell_features.shape[1:])


def on_device(
    orbitals, v_local, features, w_first, w_hidden, w_last, rotation, assignment, degrees
):
    group = lax.axis_index("band")
    local_slots, size_x, size_y, size_z = orbitals.shape
    total_slots = rotation.shape[0]
    cells = size_x * size_y * size_z
    total_cells = float(cells * lax.axis_size("gx") * lax.axis_size("gyz"))
    xc_field = network(features, w_first, w_hidden, w_last)
    potential = v_local + xc_field
    factors, centre = coefficients(DEG)
    previous = orbitals
    current = orbitals
    for rounds in range(DEG):
        image = hamiltonian(current, potential)
        scale_new, scale_old = factors[rounds]
        updated = scale_new * (image - centre * current) - scale_old * previous
        active = (degrees > rounds)[:, None, None, None]
        previous = jnp.where(active, current, previous)
        current = jnp.where(active, updated, current)
    filtered = current.astype(jnp.bfloat16).reshape(local_slots, cells)
    select = (assignment[:, None] == lax.iota(jnp.int32, total_slots)[None, :]).astype(jnp.float32)
    permuted = jnp.dot(select, rotation, precision=lax.Precision.HIGHEST)
    slot_rotation = jnp.dot(permuted, select.T, precision=lax.Precision.HIGHEST).astype(
        jnp.bfloat16
    )
    own_columns = lax.dynamic_slice_in_dim(slot_rotation, group * local_slots, local_slots, 1)
    shard_rows = lax.all_gather(filtered, "band", axis=0, tiled=True)
    margin = lax.dot_general(
        filtered, shard_rows, (((1,), (1,)), ((), ())), preferred_element_type=jnp.float32
    )
    gram_part = margin
    rotated_part = lax.dot_general(
        own_columns, shard_rows, (((0,), (0,)), ((), ())), preferred_element_type=jnp.float32
    )
    gram_part, rotated_flat = (gram_part, rotated_part)
    gram = lax.psum(gram_part, ("gx", "gyz")) / total_cells
    rotated = rotated_flat.reshape(local_slots, size_x, size_y, size_z)
    return (gram, rotated)


def solution(mesh):
    placed = (
        P("band", "gx", "gyz", None),
        P("gx", "gyz", None),
        P(None, "gx", "gyz", None),
        P(),
        P(),
        P(),
        P(),
        P(),
        P("band"),
    )
    return jax.shard_map(
        on_device,
        mesh=mesh,
        in_specs=placed,
        out_specs=(P("band", None), P("band", "gx", "gyz", None)),
        check_vma=False,
    )
```

profile of v0, /device:TPU:8, one launch (start us, length us, event | category | flops | bytes accessed | tf_op | source)
XLA Modules:
  0.0 750.5 jit_solution(973591448265603997)
XLA Ops:
  7.2 1.9 copy.25
  9.1 1.8 collective-permute-start.1
  13.8 3.4 multiply_convert_fusion.1
  17.3 3.3 fusion.1
  21.3 3.7 collective-permute-start.2
  25.1 2.1 collective-permute-start.3
  27.2 2.1 collective-permute-done.2
  29.3 6.6 collective-permute-done.3
  39.2 3.0 collective-permute-start.5
  43.4 2.0 collective-permute-start.6
  45.5 3.8 collective-permute-start.7
  49.3 1.7 collective-permute-done.6
  51.0 3.5 collective-permute-done.7
  54.5 2.1 select_maximum_fusion.24
  59.2 4.8 collective-permute-start.9
  65.1 1.9 collective-permute-start.10
  67.1 3.9 collective-permute-start.11
  72.7 4.7 collective-permute-done.11
  77.4 2.1 select_maximum_fusion.20
  82.6 5.3 collective-permute-start.13
  89.0 1.9 collective-permute-start.14
  91.0 4.1 collective-permute-start.15
  96.6 4.7 collective-permute-done.15
  101.3 2.1 select_maximum_fusion.16
  103.5 1.8 fusion.49
  106.7 5.3 collective-permute-start.17
  113.1 1.9 collective-permute-start.18
  115.0 3.9 collective-permute-start.19
  120.7 4.7 collective-permute-done.19
  125.4 2.1 select_maximum_fusion.12
  130.1 5.3 collective-permute-start.21
  136.6 1.9 collective-permute-start.22
  138.5 3.9 collective-permute-start.23
  144.2 4.7 collective-permute-done.23
  148.9 2.1 select_maximum_fusion.8
  154.0 5.3 collective-permute-start.25
  160.4 1.9 collective-permute-start.26
  162.3 3.9 collective-permute-start.27
  168.0 4.7 collective-permute-done.27
  172.7 2.1 select_maximum_fusion.4
  177.4 5.3 collective-permute-start.29
  183.9 1.9 collective-permute-start.30
  185.8 3.9 collective-permute-start.31
  191.4 4.7 collective-permute-done.31
  196.2 2.1 select_maximum_fusion
  201.8 60.9 %all-gather.2.cloned.1.call-done = bf16[256,4096]{1,0:T(8,128)(2,1)} async-done(((bf16[64,4096]{1,0:T(8,128)(2,1)}), bf16[256,4096]{1,0:T(8,128)(2,1)}) %all-gather.2.cloned.1.call-update) | async-done | bytes 2097168 | tf_op jit(solution)/shard_map/all_gather | solution.py:87
  262.7 3.2 fusion.91
  267.6 474.6 %all-reduce.10.cloned.1.call-done = f32[64,256]{1,0:T(8,128)} async-done(((f32[64,256]{1,0:T(8,128)}), f32[64,256]{1,0:T(8,128)}) %all-reduce.10.cloned.1.call-update) | async-done | bytes 65552 | tf_op jit(solution)/shard_map/psum | solution.py:96
  (85 shorter events, 46.5 us)
Async XLA Ops:
  7.2 194.0 %copy-start = (f32[256,256]{1,0:T(8,128)S(1)}, f32[256,256]{1,0:T(8,128)}, u32[]{:S(2)}) copy-start(f32[256,256]{1,0:T(8,128)} %param.15) | copy-start | bytes 786436
  7.2 255.5 %all-gather.2.cloned.1.call-start = ((), (), s32[]{:S(2)}) async-start(), calls=%async_computation | async-start | bytes 2621440 | tf_op jit(solution)/shard_map/all_gather | solution.py:87
  9.1 11.5 %collective-permute-start.1 = (f32[64,1,8,128]{3,0,2,1:T(8,128)S(1)}, f32[64,1,8,128]{3,0,2,1:T(8,128)S(1)}, u32[]{:S(2)}, u32[]{:S(2)}) collective-permute-start(f32[64,1,8,128]{3,0,2,1:T(8,128)S(1)} %get-tuple-element.37), channel_id=1, source_target_pairs={{0,32},{32,64},{64,96},{96,128},{128,160},{160,192},{192,224},{1,3... | collective-permute-start | bytes 786440 | tf_op jit(solution)/shard_map/ppermute | solution.py:17
  10.9 10.4 %collective-permute-start = (f32[64,1,8,128]{3,0,2,1:T(8,128)S(1)}, f32[64,1,8,128]{3,0,2,1:T(8,128)S(1)}, u32[]{:S(2)}, u32[]{:S(2)}) collective-permute-start(f32[64,1,8,128]{3,0,2,1:T(8,128)S(1)} %get-tuple-element.36), channel_id=1, source_target_pairs={{32,0},{64,32},{96,64},{128,96},{160,128},{192,160},{224,192},{33,... | collective-permute-start | bytes 786440 | tf_op jit(solution)/shard_map/ppermute | solution.py:20
  17.3 3.3 copy-start.3
  17.3 3.4 copy-start.1
  20.6 6.6 copy-start.5
  21.3 8.0 %collective-permute-start.2 = (f32[64,6,1,128]{3,0,2,1:T(8,128)S(1)}, f32[64,6,1,128]{3,0,2,1:T(8,128)S(1)}, u32[]{:S(2)}, u32[]{:S(2)}) collective-permute-start(f32[64,6,1,128]{3,0,2,1:T(8,128)S(1)} %get-tuple-element.21), channel_id=1, source_target_pairs={{4,0},{8,4},{12,8},{16,12},{20,16},{24,20},{28,24},{5,1},{9,5},{13... | collective-permute-start | bytes 589832 | tf_op jit(solution)/shard_map/ppermute | solution.py:20
  25.1 10.9 %collective-permute-start.3 = (f32[64,6,1,128]{3,0,2,1:T(8,128)S(1)}, f32[64,6,1,128]{3,0,2,1:T(8,128)S(1)}, u32[]{:S(2)}, u32[]{:S(2)}) collective-permute-start(f32[64,6,1,128]{3,0,2,1:T(8,128)S(1)} %get-tuple-element.20), channel_id=1, source_target_pairs={{0,4},{4,8},{8,12},{12,16},{16,20},{20,24},{24,28},{1,5},{5,9},{9,... | collective-permute-start | bytes 589832 | tf_op jit(solution)/shard_map/ppermute | solution.py:17
  37.9 4.4 collective-permute-start.4
  39.2 4.2 collective-permute-start.5
  43.4 7.6 %collective-permute-start.6 = (f32[64,6,1,128]{3,0,2,1:T(8,128)S(1)}, f32[64,6,1,128]{3,0,2,1:T(8,128)S(1)}, u32[]{:S(2)}, u32[]{:S(2)}) collective-permute-start(f32[64,6,1,128]{3,0,2,1:T(8,128)S(1)} %get-tuple-element.19), channel_id=1, source_target_pairs={{4,0},{8,4},{12,8},{16,12},{20,16},{24,20},{28,24},{5,1},{9,5},{13... | collective-permute-start | bytes 589832 | tf_op jit(solution)/shard_map/ppermute | solution.py:20
  45.5 9.0 %collective-permute-start.7 = (f32[64,6,1,128]{3,0,2,1:T(8,128)S(1)}, f32[64,6,1,128]{3,0,2,1:T(8,128)S(1)}, u32[]{:S(2)}, u32[]{:S(2)}) collective-permute-start(f32[64,6,1,128]{3,0,2,1:T(8,128)S(1)} %get-tuple-element.18), channel_id=1, source_target_pairs={{0,4},{4,8},{8,12},{12,16},{16,20},{20,24},{24,28},{1,5},{5,9},{9,... | collective-permute-start | bytes 589832 | tf_op jit(solution)/shard_map/ppermute | solution.py:17
  57.9 6.1 collective-permute-start.8
  59.2 5.9 collective-permute-start.9
  65.1 7.6 %collective-permute-start.10 = (f32[64,6,1,128]{3,0,2,1:T(8,128)S(1)}, f32[64,6,1,128]{3,0,2,1:T(8,128)S(1)}, u32[]{:S(2)}, u32[]{:S(2)}) collective-permute-start(f32[64,6,1,128]{3,0,2,1:T(8,128)S(1)} %get-tuple-element.17), channel_id=1, source_target_pairs={{4,0},{8,4},{12,8},{16,12},{20,16},{24,20},{28,24},{5,1},{9,5},{13... | collective-permute-start | bytes 589832 | tf_op jit(solution)/shard_map/ppermute | solution.py:20
  67.1 10.4 %collective-permute-start.11 = (f32[64,6,1,128]{3,0,2,1:T(8,128)S(1)}, f32[64,6,1,128]{3,0,2,1:T(8,128)S(1)}, u32[]{:S(2)}, u32[]{:S(2)}) collective-permute-start(f32[64,6,1,128]{3,0,2,1:T(8,128)S(1)} %get-tuple-element.16), channel_id=1, source_target_pairs={{0,4},{4,8},{8,12},{12,16},{16,20},{20,24},{24,28},{1,5},{5,9},{9,... | collective-permute-start | bytes 589832 | tf_op jit(solution)/shard_map/ppermute | solution.py:17
  81.3 6.6 collective-permute-start.12
  82.6 6.4 collective-permute-start.13
  89.0 7.6 %collective-permute-start.14 = (f32[64,6,1,128]{3,0,2,1:T(8,128)S(1)}, f32[64,6,1,128]{3,0,2,1:T(8,128)S(1)}, u32[]{:S(2)}, u32[]{:S(2)}) collective-permute-start(f32[64,6,1,128]{3,0,2,1:T(8,128)S(1)} %get-tuple-element.15), channel_id=1, source_target_pairs={{4,0},{8,4},{12,8},{16,12},{20,16},{24,20},{28,24},{5,1},{9,5},{13... | collective-permute-start | bytes 589832 | tf_op jit(solution)/shard_map/ppermute | solution.py:20
  91.0 10.4 %collective-permute-start.15 = (f32[64,6,1,128]{3,0,2,1:T(8,128)S(1)}, f32[64,6,1,128]{3,0,2,1:T(8,128)S(1)}, u32[]{:S(2)}, u32[]{:S(2)}) collective-permute-start(f32[64,6,1,128]{3,0,2,1:T(8,128)S(1)} %get-tuple-element.14), channel_id=1, source_target_pairs={{0,4},{4,8},{8,12},{12,16},{16,20},{20,24},{24,28},{1,5},{5,9},{9,... | collective-permute-start | bytes 589832 | tf_op jit(solution)/shard_map/ppermute | solution.py:17
  105.4 6.6 collective-permute-start.16
  106.7 6.4 collective-permute-start.17
  113.1 7.6 %collective-permute-start.18 = (f32[64,6,1,128]{3,0,2,1:T(8,128)S(1)}, f32[64,6,1,128]{3,0,2,1:T(8,128)S(1)}, u32[]{:S(2)}, u32[]{:S(2)}) collective-permute-start(f32[64,6,1,128]{3,0,2,1:T(8,128)S(1)} %get-tuple-element.13), channel_id=1, source_target_pairs={{4,0},{8,4},{12,8},{16,12},{20,16},{24,20},{28,24},{5,1},{9,5},{13... | collective-permute-start | bytes 589832 | tf_op jit(solution)/shard_map/ppermute | solution.py:20
  115.0 10.4 %collective-permute-start.19 = (f32[64,6,1,128]{3,0,2,1:T(8,128)S(1)}, f32[64,6,1,128]{3,0,2,1:T(8,128)S(1)}, u32[]{:S(2)}, u32[]{:S(2)}) collective-permute-start(f32[64,6,1,128]{3,0,2,1:T(8,128)S(1)} %get-tuple-element.12), channel_id=1, source_target_pairs={{0,4},{4,8},{8,12},{12,16},{16,20},{20,24},{24,28},{1,5},{5,9},{9,... | collective-permute-start | bytes 589832 | tf_op jit(solution)/shard_map/ppermute | solution.py:17
  128.8 6.6 collective-permute-start.20
  130.1 6.4 collective-permute-start.21
  136.6 7.6 %collective-permute-start.22 = (f32[64,6,1,128]{3,0,2,1:T(8,128)S(1)}, f32[64,6,1,128]{3,0,2,1:T(8,128)S(1)}, u32[]{:S(2)}, u32[]{:S(2)}) collective-permute-start(f32[64,6,1,128]{3,0,2,1:T(8,128)S(1)} %get-tuple-element.11), channel_id=1, source_target_pairs={{4,0},{8,4},{12,8},{16,12},{20,16},{24,20},{28,24},{5,1},{9,5},{13... | collective-permute-start | bytes 589832 | tf_op jit(solution)/shard_map/ppermute | solution.py:20
  138.5 10.4 %collective-permute-start.23 = (f32[64,6,1,128]{3,0,2,1:T(8,128)S(1)}, f32[64,6,1,128]{3,0,2,1:T(8,128)S(1)}, u32[]{:S(2)}, u32[]{:S(2)}) collective-permute-start(f32[64,6,1,128]{3,0,2,1:T(8,128)S(1)} %get-tuple-element.10), channel_id=1, source_target_pairs={{0,4},{4,8},{8,12},{12,16},{16,20},{20,24},{24,28},{1,5},{5,9},{9,... | collective-permute-start | bytes 589832 | tf_op jit(solution)/shard_map/ppermute | solution.py:17
  152.7 6.6 collective-permute-start.24
  154.0 6.4 collective-permute-start.25
  160.4 7.6 %collective-permute-start.26 = (f32[64,6,1,128]{3,0,2,1:T(8,128)S(1)}, f32[64,6,1,128]{3,0,2,1:T(8,128)S(1)}, u32[]{:S(2)}, u32[]{:S(2)}) collective-permute-start(f32[64,6,1,128]{3,0,2,1:T(8,128)S(1)} %get-tuple-element.9), channel_id=1, source_target_pairs={{4,0},{8,4},{12,8},{16,12},{20,16},{24,20},{28,24},{5,1},{9,5},{13... | collective-permute-start | bytes 589832 | tf_op jit(solution)/shard_map/ppermute | solution.py:20
  162.3 10.4 %collective-permute-start.27 = (f32[64,6,1,128]{3,0,2,1:T(8,128)S(1)}, f32[64,6,1,128]{3,0,2,1:T(8,128)S(1)}, u32[]{:S(2)}, u32[]{:S(2)}) collective-permute-start(f32[64,6,1,128]{3,0,2,1:T(8,128)S(1)} %get-tuple-element.8), channel_id=1, source_target_pairs={{0,4},{4,8},{8,12},{12,16},{16,20},{20,24},{24,28},{1,5},{5,9},{9,... | collective-permute-start | bytes 589832 | tf_op jit(solution)/shard_map/ppermute | solution.py:17
  176.1 6.6 collective-permute-start.28
  177.4 6.4 collective-permute-start.29
  183.9 7.6 %collective-permute-start.30 = (f32[64,6,1,128]{3,0,2,1:T(8,128)S(1)}, f32[64,6,1,128]{3,0,2,1:T(8,128)S(1)}, u32[]{:S(2)}, u32[]{:S(2)}) collective-permute-start(f32[64,6,1,128]{3,0,2,1:T(8,128)S(1)} %get-tuple-element.7), channel_id=1, source_target_pairs={{4,0},{8,4},{12,8},{16,12},{20,16},{24,20},{28,24},{5,1},{9,5},{13... | collective-permute-start | bytes 589832 | tf_op jit(solution)/shard_map/ppermute | solution.py:20
  185.8 10.4 %collective-permute-start.31 = (f32[64,6,1,128]{3,0,2,1:T(8,128)S(1)}, f32[64,6,1,128]{3,0,2,1:T(8,128)S(1)}, u32[]{:S(2)}, u32[]{:S(2)}) collective-permute-start(f32[64,6,1,128]{3,0,2,1:T(8,128)S(1)} %get-tuple-element.6), channel_id=1, source_target_pairs={{0,4},{4,8},{8,12},{12,16},{16,20},{20,24},{24,28},{1,5},{5,9},{9,... | collective-permute-start | bytes 589832 | tf_op jit(solution)/shard_map/ppermute | solution.py:17
  198.3 2.8 copy-start.4
  201.1 541.1 %all-reduce.10.cloned.1.call-start = ((), (), s32[]{:S(2)}) async-start(), calls=%async_computation.1 | async-start | bytes 131072 | tf_op jit(solution)/shard_map/psum | solution.py:96
  262.7 3.2 copy-start.2
Sparse Core Ops, SparseCore 0:
  201.2 61.4 all-gather.1
  266.0 476.0 all-reduce.9
where the time goes:
time: 752 us; the launch traced here: 750 us
  waiting for transfers between devices  596 us (79%)
  starting transfers between devices  93.3 us (12%)
  other arithmetic  28.6 us (4%)
  between operations  14.7 us (2%)
  matrix products  11 us (1%)
    psum x1, waiting for transfers between devices, on_device(): gram = lax.psum(gram_part, ('gx', 'gyz')) / total_cells  475 us
    ppermute x16, starting transfers between devices, with_halo(): lax.ppermute(lax.slice_in_dim(block, block.shape[dim] - width, None, axis...  65.6 us
    all_gather x1, waiting for transfers between devices, on_device(): shard_rows = lax.all_gather(filtered, 'band', axis=0, tiled=True)  60.9 us
    ppermute x16, waiting for transfers between devices, with_halo(): lax.ppermute(lax.slice_in_dim(block, block.shape[dim] - width, None, axis...  46.3 us
    ppermute x16, starting transfers between devices, with_halo(): lax.ppermute(lax.slice_in_dim(block, 0, width, axis=dim), axis, backward)  27.6 us
    concatenate x15, other arithmetic, with_halo(): block = jnp.concatenate([low, block, high], axis=dim)  16.2 us
  transfers between devices with their start and end apart: 34, of which 25 were waited for; matrix products, arithmetic and copies ran while one was open for 2% of the time, Pallas kernels for 0%

commit v1 on v0

--- a/solution.py
+++ b/solution.py
@@ -7,6 +7,12 @@
 LOWER_EDGE = 2.0
 CUT_EDGE = 3.0
 UPPER_EDGE = 9.5
+
+
+def pair_chains(array_in):
+    local_part = lax.all_gather(array_in, ("gx", "gyz"))
+    main = jnp.sum(local_part, axis=0)
+    return main
 
 
 def with_halo(block, sides, width):
@@ -93,7 +99,7 @@
         own_columns, shard_rows, (((0,), (0,)), ((), ())), preferred_element_type=jnp.float32
     )
     gram_part, rotated_flat = (gram_part, rotated_part)
-    gram = lax.psum(gram_part, ("gx", "gyz")) / total_cells
+    gram = pair_chains(gram_part) / total_cells
     rotated = rotated_flat.reshape(local_slots, size_x, size_y, size_z)
     return (gram, rotated)
 

time: 752 us -> 440 us (0.59)
  waiting for transfers between devices: 596 us -> 279 us
    psum x1 -> x0, waiting for transfers between devices: 475 us -> none  [on_device(): gram = lax.psum(gram_part, ('gx', 'gyz')) / total_cells]
    all_gather x0 -> x1, waiting for transfers between devices: none -> 157 us  [pair_chains(): local_part = lax.all_gather(array_in, ('gx', 'gyz'))]
  transfers between devices with their start and end apart: 34 -> 34, of which waited for: 25 -> 25; matrix products, arithmetic and copies ran while one was open for 2% -> 3% of each run, Pallas kernels for 0% -> 0%
where the time goes in v1:
time: 440 us; the launch traced here: 435 us
  waiting for transfers between devices  279 us (63%)
  starting transfers between devices  93.3 us (21%)
  other arithmetic  30.2 us (7%)
  between operations  14.7 us (3%)
  matrix products  11 us (2%)
  local copies, waits for them, and re-layouts  7.04 us (2%)
    all_gather x1, waiting for transfers between devices, pair_chains(): local_part = lax.all_gather(array_in, ('gx', 'gyz'))  157 us
    ppermute x16, starting transfers between devices, with_halo(): lax.ppermute(lax.slice_in_dim(block, block.shape[dim] - width, None, axis...  65.6 us
    all_gather x1, waiting for transfers between devices, on_device(): shard_rows = lax.all_gather(filtered, 'band', axis=0, tiled=True)  61.6 us
    ppermute x16, waiting for transfers between devices, with_halo(): lax.ppermute(lax.slice_in_dim(block, block.shape[dim] - width, None, axis...  46.3 us
    ppermute x16, starting transfers between devices, with_halo(): lax.ppermute(lax.slice_in_dim(block, 0, width, axis=dim), axis, backward)  27.6 us
    concatenate x15, other arithmetic, with_halo(): block = jnp.concatenate([low, block, high], axis=dim)  16.2 us
    ppermute x16, waiting for transfers between devices, with_halo(): lax.ppermute(lax.slice_in_dim(block, 0, width, axis=dim), axis, backward)  13.9 us
    select_n x7, other arithmetic, on_device(): current = jnp.where(active, updated, current)  9.57 us
  transfers between devices with their start and end apart: 34, of which 25 were waited for; matrix products, arithmetic and copies ran while one was open for 3% of the time, Pallas kernels for 0%

profile of v1, /device:TPU:8, one launch (start us, length us, event | category | flops | bytes accessed | tf_op | source)
XLA Modules:
  0.0 435.2 jit_solution(18297733305660152088)
XLA Ops:
  7.2 1.9 copy.25
  9.1 1.8 collective-permute-start.1
  13.8 3.4 multiply_convert_fusion.1
  17.3 3.3 fusion.1
  21.3 3.7 collective-permute-start.2
  25.1 2.1 collective-permute-start.3
  27.2 2.1 collective-permute-done.2
  29.3 6.6 %collective-permute-done.3 = f32[64,6,1,128]{3,0,2,1:T(8,128)S(1)} collective-permute-done((f32[64,6,1,128]{3,0,2,1:T(8,128)S(1)}, f32[64,6,1,128]{3,0,2,1:T(8,128)S(1)}, u32[]{:S(2)}, u32[]{:S(2)}) %collective-permute-start.3) | collective-permute-done | bytes 196640 | tf_op jit(solution)/shard_map/ppermute | solution.py:23
  39.2 3.0 collective-permute-start.5
  43.4 2.0 collective-permute-start.6
  45.5 3.8 collective-permute-start.7
  51.0 3.5 collective-permute-done.7
  54.5 2.1 select_maximum_fusion.24
  59.2 4.8 %collective-permute-start.9 = (f32[64,1,8,128]{3,0,2,1:T(8,128)S(1)}, f32[64,1,8,128]{3,0,2,1:T(8,128)S(1)}, u32[]{:S(2)}, u32[]{:S(2)}) collective-permute-start(f32[64,1,8,128]{3,0,2,1:T(8,128)S(1)} %get-tuple-element.32), channel_id=1, source_target_pairs={{0,32},{32,64},{64,96},{96,128},{128,160},{160,192},{192,224},{1,3... | collective-permute-start | bytes 786440 | tf_op jit(solution)/shard_map/ppermute | solution.py:23
  65.1 1.9 collective-permute-start.10
  67.1 3.9 collective-permute-start.11
  72.7 4.7 %collective-permute-done.11 = f32[64,6,1,128]{3,0,2,1:T(8,128)S(1)} collective-permute-done((f32[64,6,1,128]{3,0,2,1:T(8,128)S(1)}, f32[64,6,1,128]{3,0,2,1:T(8,128)S(1)}, u32[]{:S(2)}, u32[]{:S(2)}) %collective-permute-start.11) | collective-permute-done | bytes 196640 | tf_op jit(solution)/shard_map/ppermute | solution.py:23
  77.4 2.1 select_maximum_fusion.20
  82.6 5.3 %collective-permute-start.13 = (f32[64,1,8,128]{3,0,2,1:T(8,128)S(1)}, f32[64,1,8,128]{3,0,2,1:T(8,128)S(1)}, u32[]{:S(2)}, u32[]{:S(2)}) collective-permute-start(f32[64,1,8,128]{3,0,2,1:T(8,128)S(1)} %get-tuple-element.30), channel_id=1, source_target_pairs={{0,32},{32,64},{64,96},{96,128},{128,160},{160,192},{192,224},{1,3... | collective-permute-start | bytes 786440 | tf_op jit(solution)/shard_map/ppermute | solution.py:23
  89.0 1.9 collective-permute-start.14
  91.0 4.1 collective-permute-start.15
  96.6 4.7 %collective-permute-done.15 = f32[64,6,1,128]{3,0,2,1:T(8,128)S(1)} collective-permute-done((f32[64,6,1,128]{3,0,2,1:T(8,128)S(1)}, f32[64,6,1,128]{3,0,2,1:T(8,128)S(1)}, u32[]{:S(2)}, u32[]{:S(2)}) %collective-permute-start.15) | collective-permute-done | bytes 196640 | tf_op jit(solution)/shard_map/ppermute | solution.py:23
  101.3 2.1 select_maximum_fusion.16
  103.5 1.8 fusion.49
  106.7 5.3 %collective-permute-start.17 = (f32[64,1,8,128]{3,0,2,1:T(8,128)S(1)}, f32[64,1,8,128]{3,0,2,1:T(8,128)S(1)}, u32[]{:S(2)}, u32[]{:S(2)}) collective-permute-start(f32[64,1,8,128]{3,0,2,1:T(8,128)S(1)} %get-tuple-element.28), channel_id=1, source_target_pairs={{0,32},{32,64},{64,96},{96,128},{128,160},{160,192},{192,224},{1,3... | collective-permute-start | bytes 786440 | tf_op jit(solution)/shard_map/ppermute | solution.py:23
  113.1 1.9 collective-permute-start.18
  115.0 3.9 collective-permute-start.19
  120.7 4.7 %collective-permute-done.19 = f32[64,6,1,128]{3,0,2,1:T(8,128)S(1)} collective-permute-done((f32[64,6,1,128]{3,0,2,1:T(8,128)S(1)}, f32[64,6,1,128]{3,0,2,1:T(8,128)S(1)}, u32[]{:S(2)}, u32[]{:S(2)}) %collective-permute-start.19) | collective-permute-done | bytes 196640 | tf_op jit(solution)/shard_map/ppermute | solution.py:23
  125.4 2.1 select_maximum_fusion.12
  130.1 5.3 %collective-permute-start.21 = (f32[64,1,8,128]{3,0,2,1:T(8,128)S(1)}, f32[64,1,8,128]{3,0,2,1:T(8,128)S(1)}, u32[]{:S(2)}, u32[]{:S(2)}) collective-permute-start(f32[64,1,8,128]{3,0,2,1:T(8,128)S(1)} %get-tuple-element.26), channel_id=1, source_target_pairs={{0,32},{32,64},{64,96},{96,128},{128,160},{160,192},{192,224},{1,3... | collective-permute-start | bytes 786440 | tf_op jit(solution)/shard_map/ppermute | solution.py:23
  136.6 1.9 collective-permute-start.22
  138.5 3.9 collective-permute-start.23
  144.2 4.7 %collective-permute-done.23 = f32[64,6,1,128]{3,0,2,1:T(8,128)S(1)} collective-permute-done((f32[64,6,1,128]{3,0,2,1:T(8,128)S(1)}, f32[64,6,1,128]{3,0,2,1:T(8,128)S(1)}, u32[]{:S(2)}, u32[]{:S(2)}) %collective-permute-start.23) | collective-permute-done | bytes 196640 | tf_op jit(solution)/shard_map/ppermute | solution.py:23
  148.9 2.1 select_maximum_fusion.8
  154.0 5.3 %collective-permute-start.25 = (f32[64,1,8,128]{3,0,2,1:T(8,128)S(1)}, f32[64,1,8,128]{3,0,2,1:T(8,128)S(1)}, u32[]{:S(2)}, u32[]{:S(2)}) collective-permute-start(f32[64,1,8,128]{3,0,2,1:T(8,128)S(1)} %get-tuple-element.24), channel_id=1, source_target_pairs={{0,32},{32,64},{64,96},{96,128},{128,160},{160,192},{192,224},{1,3... | collective-permute-start | bytes 786440 | tf_op jit(solution)/shard_map/ppermute | solution.py:23
  160.4 1.9 collective-permute-start.26
  162.3 3.9 collective-permute-start.27
  168.0 4.7 %collective-permute-done.27 = f32[64,6,1,128]{3,0,2,1:T(8,128)S(1)} collective-permute-done((f32[64,6,1,128]{3,0,2,1:T(8,128)S(1)}, f32[64,6,1,128]{3,0,2,1:T(8,128)S(1)}, u32[]{:S(2)}, u32[]{:S(2)}) %collective-permute-start.27) | collective-permute-done | bytes 196640 | tf_op jit(solution)/shard_map/ppermute | solution.py:23
  172.7 2.1 select_maximum_fusion.4
  177.4 5.3 %collective-permute-start.29 = (f32[64,1,8,128]{3,0,2,1:T(8,128)S(1)}, f32[64,1,8,128]{3,0,2,1:T(8,128)S(1)}, u32[]{:S(2)}, u32[]{:S(2)}) collective-permute-start(f32[64,1,8,128]{3,0,2,1:T(8,128)S(1)} %get-tuple-element.22), channel_id=1, source_target_pairs={{0,32},{32,64},{64,96},{96,128},{128,160},{160,192},{192,224},{1,3... | collective-permute-start | bytes 786440 | tf_op jit(solution)/shard_map/ppermute | solution.py:23
  183.9 1.9 collective-permute-start.30
  185.8 3.9 collective-permute-start.31
  191.4 4.7 %collective-permute-done.31 = f32[64,6,1,128]{3,0,2,1:T(8,128)S(1)} collective-permute-done((f32[64,6,1,128]{3,0,2,1:T(8,128)S(1)}, f32[64,6,1,128]{3,0,2,1:T(8,128)S(1)}, u32[]{:S(2)}, u32[]{:S(2)}) %collective-permute-start.31) | collective-permute-done | bytes 196640 | tf_op jit(solution)/shard_map/ppermute | solution.py:23
  196.2 2.1 select_maximum_fusion
  201.1 61.6 %all-gather.4.cloned.1.call-done = bf16[256,4096]{1,0:T(8,128)(2,1)} async-done(((bf16[64,4096]{1,0:T(8,128)(2,1)}), bf16[256,4096]{1,0:T(8,128)(2,1)}) %all-gather.4.cloned.1.call-update) | async-done | bytes 2097168 | tf_op jit(solution)/shard_map/all_gather | solution.py:93
  262.7 3.2 fusion.91
  268.3 157.0 %all-gather.6.cloned.1.call-done = f32[4096,256]{1,0:T(8,128)} async-done(((f32[64,256]{1,0:T(8,128)}), f32[4096,256]{1,0:T(8,128)}) %all-gather.6.cloned.1.call-update) | async-done | bytes 4194320 | tf_op jit(solution)/shard_map/all_gather | solution.py:13
  425.2 2.4 reduce_sum.9
  (86 shorter events, 47.4 us)
Async XLA Ops:
  7.2 258.8 %copy-start = (f32[256,256]{1,0:T(8,128)S(1)}, f32[256,256]{1,0:T(8,128)}, u32[]{:S(2)}) copy-start(f32[256,256]{1,0:T(8,128)} %param.15) | copy-start | bytes 786436
  7.2 255.5 %all-gather.4.cloned.1.call-start = ((), (), s32[]{:S(2)}) async-start(), calls=%async_computation | async-start | bytes 2621440 | tf_op jit(solution)/shard_map/all_gather | solution.py:93
  9.1 11.5 %collective-permute-start.1 = (f32[64,1,8,128]{3,0,2,1:T(8,128)S(1)}, f32[64,1,8,128]{3,0,2,1:T(8,128)S(1)}, u32[]{:S(2)}, u32[]{:S(2)}) collective-permute-start(f32[64,1,8,128]{3,0,2,1:T(8,128)S(1)} %get-tuple-element.37), channel_id=1, source_target_pairs={{0,32},{32,64},{64,96},{96,128},{128,160},{160,192},{192,224},{1,3... | collective-permute-start | bytes 786440 | tf_op jit(solution)/shard_map/ppermute | solution.py:23
  10.9 10.4 %collective-permute-start = (f32[64,1,8,128]{3,0,2,1:T(8,128)S(1)}, f32[64,1,8,128]{3,0,2,1:T(8,128)S(1)}, u32[]{:S(2)}, u32[]{:S(2)}) collective-permute-start(f32[64,1,8,128]{3,0,2,1:T(8,128)S(1)} %get-tuple-element.36), channel_id=1, source_target_pairs={{32,0},{64,32},{96,64},{128,96},{160,128},{192,160},{224,192},{33,... | collective-permute-start | bytes 786440 | tf_op jit(solution)/shard_map/ppermute | solution.py:26
  17.3 3.3 copy-start.3
  17.3 3.4 copy-start.1
  20.6 6.6 %copy-start.5 = (s32[64]{0:T(128)S(1)}, s32[64]{0:T(128)}, u32[]{:S(2)}) copy-start(s32[64]{0:T(128)} %param.17) | copy-start | bytes 772
  21.3 8.0 %collective-permute-start.2 = (f32[64,6,1,128]{3,0,2,1:T(8,128)S(1)}, f32[64,6,1,128]{3,0,2,1:T(8,128)S(1)}, u32[]{:S(2)}, u32[]{:S(2)}) collective-permute-start(f32[64,6,1,128]{3,0,2,1:T(8,128)S(1)} %get-tuple-element.21), channel_id=1, source_target_pairs={{4,0},{8,4},{12,8},{16,12},{20,16},{24,20},{28,24},{5,1},{9,5},{13... | collective-permute-start | bytes 589832 | tf_op jit(solution)/shard_map/ppermute | solution.py:26
  25.1 10.9 %collective-permute-start.3 = (f32[64,6,1,128]{3,0,2,1:T(8,128)S(1)}, f32[64,6,1,128]{3,0,2,1:T(8,128)S(1)}, u32[]{:S(2)}, u32[]{:S(2)}) collective-permute-start(f32[64,6,1,128]{3,0,2,1:T(8,128)S(1)} %get-tuple-element.20), channel_id=1, source_target_pairs={{0,4},{4,8},{8,12},{12,16},{16,20},{20,24},{24,28},{1,5},{5,9},{9,... | collective-permute-start | bytes 589832 | tf_op jit(solution)/shard_map/ppermute | solution.py:23
  37.9 4.4 %collective-permute-start.4 = (f32[64,1,8,128]{3,0,2,1:T(8,128)S(1)}, f32[64,1,8,128]{3,0,2,1:T(8,128)S(1)}, u32[]{:S(2)}, u32[]{:S(2)}) collective-permute-start(f32[64,1,8,128]{3,0,2,1:T(8,128)S(1)} %get-tuple-element.35), channel_id=1, source_target_pairs={{32,0},{64,32},{96,64},{128,96},{160,128},{192,160},{224,192},{33,... | collective-permute-start | bytes 786440 | tf_op jit(solution)/shard_map/ppermute | solution.py:26
  39.2 4.2 collective-permute-start.5
  43.4 7.6 %collective-permute-start.6 = (f32[64,6,1,128]{3,0,2,1:T(8,128)S(1)}, f32[64,6,1,128]{3,0,2,1:T(8,128)S(1)}, u32[]{:S(2)}, u32[]{:S(2)}) collective-permute-start(f32[64,6,1,128]{3,0,2,1:T(8,128)S(1)} %get-tuple-element.19), channel_id=1, source_target_pairs={{4,0},{8,4},{12,8},{16,12},{20,16},{24,20},{28,24},{5,1},{9,5},{13... | collective-permute-start | bytes 589832 | tf_op jit(solution)/shard_map/ppermute | solution.py:26
  45.5 9.0 %collective-permute-start.7 = (f32[64,6,1,128]{3,0,2,1:T(8,128)S(1)}, f32[64,6,1,128]{3,0,2,1:T(8,128)S(1)}, u32[]{:S(2)}, u32[]{:S(2)}) collective-permute-start(f32[64,6,1,128]{3,0,2,1:T(8,128)S(1)} %get-tuple-element.18), channel_id=1, source_target_pairs={{0,4},{4,8},{8,12},{12,16},{16,20},{20,24},{24,28},{1,5},{5,9},{9,... | collective-permute-start | bytes 589832 | tf_op jit(solution)/shard_map/ppermute | solution.py:23
  57.9 6.1 %collective-permute-start.8 = (f32[64,1,8,128]{3,0,2,1:T(8,128)S(1)}, f32[64,1,8,128]{3,0,2,1:T(8,128)S(1)}, u32[]{:S(2)}, u32[]{:S(2)}) collective-permute-start(f32[64,1,8,128]{3,0,2,1:T(8,128)S(1)} %get-tuple-element.33), channel_id=1, source_target_pairs={{32,0},{64,32},{96,64},{128,96},{160,128},{192,160},{224,192},{33,... | collective-permute-start | bytes 786440 | tf_op jit(solution)/shard_map/ppermute | solution.py:26
  59.2 5.9 %collective-permute-start.9 = (f32[64,1,8,128]{3,0,2,1:T(8,128)S(1)}, f32[64,1,8,128]{3,0,2,1:T(8,128)S(1)}, u32[]{:S(2)}, u32[]{:S(2)}) collective-permute-start(f32[64,1,8,128]{3,0,2,1:T(8,128)S(1)} %get-tuple-element.32), channel_id=1, source_target_pairs={{0,32},{32,64},{64,96},{96,128},{128,160},{160,192},{192,224},{1,3... | collective-permute-start | bytes 786440 | tf_op jit(solution)/shard_map/ppermute | solution.py:23
  65.1 7.6 %collective-permute-start.10 = (f32[64,6,1,128]{3,0,2,1:T(8,128)S(1)}, f32[64,6,1,128]{3,0,2,1:T(8,128)S(1)}, u32[]{:S(2)}, u32[]{:S(2)}) collective-permute-start(f32[64,6,1,128]{3,0,2,1:T(8,128)S(1)} %get-tuple-element.17), channel_id=1, source_target_pairs={{4,0},{8,4},{12,8},{16,12},{20,16},{24,20},{28,24},{5,1},{9,5},{13... | collective-permute-start | bytes 589832 | tf_op jit(solution)/shard_map/ppermute | solution.py:26
  67.1 10.4 %collective-permute-start.11 = (f32[64,6,1,128]{3,0,2,1:T(8,128)S(1)}, f32[64,6,1,128]{3,0,2,1:T(8,128)S(1)}, u32[]{:S(2)}, u32[]{:S(2)}) collective-permute-start(f32[64,6,1,128]{3,0,2,1:T(8,128)S(1)} %get-tuple-element.16), channel_id=1, source_target_pairs={{0,4},{4,8},{8,12},{12,16},{16,20},{20,24},{24,28},{1,5},{5,9},{9,... | collective-permute-start | bytes 589832 | tf_op jit(solution)/shard_map/ppermute | solution.py:23
  81.3 6.6 %collective-permute-start.12 = (f32[64,1,8,128]{3,0,2,1:T(8,128)S(1)}, f32[64,1,8,128]{3,0,2,1:T(8,128)S(1)}, u32[]{:S(2)}, u32[]{:S(2)}) collective-permute-start(f32[64,1,8,128]{3,0,2,1:T(8,128)S(1)} %get-tuple-element.31), channel_id=1, source_target_pairs={{32,0},{64,32},{96,64},{128,96},{160,128},{192,160},{224,192},{33,... | collective-permute-start | bytes 786440 | tf_op jit(solution)/shard_map/ppermute | solution.py:26
  82.6 6.4 %collective-permute-start.13 = (f32[64,1,8,128]{3,0,2,1:T(8,128)S(1)}, f32[64,1,8,128]{3,0,2,1:T(8,128)S(1)}, u32[]{:S(2)}, u32[]{:S(2)}) collective-permute-start(f32[64,1,8,128]{3,0,2,1:T(8,128)S(1)} %get-tuple-element.30), channel_id=1, source_target_pairs={{0,32},{32,64},{64,96},{96,128},{128,160},{160,192},{192,224},{1,3... | collective-permute-start | bytes 786440 | tf_op jit(solution)/shard_map/ppermute | solution.py:23
  89.0 7.6 %collective-permute-start.14 = (f32[64,6,1,128]{3,0,2,1:T(8,128)S(1)}, f32[64,6,1,128]{3,0,2,1:T(8,128)S(1)}, u32[]{:S(2)}, u32[]{:S(2)}) collective-permute-start(f32[64,6,1,128]{3,0,2,1:T(8,128)S(1)} %get-tuple-element.15), channel_id=1, source_target_pairs={{4,0},{8,4},{12,8},{16,12},{20,16},{24,20},{28,24},{5,1},{9,5},{13... | collective-permute-start | bytes 589832 | tf_op jit(solution)/shard_map/ppermute | solution.py:26
  91.0 10.4 %collective-permute-start.15 = (f32[64,6,1,128]{3,0,2,1:T(8,128)S(1)}, f32[64,6,1,128]{3,0,2,1:T(8,128)S(1)}, u32[]{:S(2)}, u32[]{:S(2)}) collective-permute-start(f32[64,6,1,128]{3,0,2,1:T(8,128)S(1)} %get-tuple-element.14), channel_id=1, source_target_pairs={{0,4},{4,8},{8,12},{12,16},{16,20},{20,24},{24,28},{1,5},{5,9},{9,... | collective-permute-start | bytes 589832 | tf_op jit(solution)/shard_map/ppermute | solution.py:23
  105.4 6.6 %collective-permute-start.16 = (f32[64,1,8,128]{3,0,2,1:T(8,128)S(1)}, f32[64,1,8,128]{3,0,2,1:T(8,128)S(1)}, u32[]{:S(2)}, u32[]{:S(2)}) collective-permute-start(f32[64,1,8,128]{3,0,2,1:T(8,128)S(1)} %get-tuple-element.29), channel_id=1, source_target_pairs={{32,0},{64,32},{96,64},{128,96},{160,128},{192,160},{224,192},{33,... | collective-permute-start | bytes 786440 | tf_op jit(solution)/shard_map/ppermute | solution.py:26
  106.7 6.4 %collective-permute-start.17 = (f32[64,1,8,128]{3,0,2,1:T(8,128)S(1)}, f32[64,1,8,128]{3,0,2,1:T(8,128)S(1)}, u32[]{:S(2)}, u32[]{:S(2)}) collective-permute-start(f32[64,1,8,128]{3,0,2,1:T(8,128)S(1)} %get-tuple-element.28), channel_id=1, source_target_pairs={{0,32},{32,64},{64,96},{96,128},{128,160},{160,192},{192,224},{1,3... | collective-permute-start | bytes 786440 | tf_op jit(solution)/shard_map/ppermute | solution.py:23
  113.1 7.6 %collective-permute-start.18 = (f32[64,6,1,128]{3,0,2,1:T(8,128)S(1)}, f32[64,6,1,128]{3,0,2,1:T(8,128)S(1)}, u32[]{:S(2)}, u32[]{:S(2)}) collective-permute-start(f32[64,6,1,128]{3,0,2,1:T(8,128)S(1)} %get-tuple-element.13), channel_id=1, source_target_pairs={{4,0},{8,4},{12,8},{16,12},{20,16},{24,20},{28,24},{5,1},{9,5},{13... | collective-permute-start | bytes 589832 | tf_op jit(solution)/shard_map/ppermute | solution.py:26
  115.0 10.4 %collective-permute-start.19 = (f32[64,6,1,128]{3,0,2,1:T(8,128)S(1)}, f32[64,6,1,128]{3,0,2,1:T(8,128)S(1)}, u32[]{:S(2)}, u32[]{:S(2)}) collective-permute-start(f32[64,6,1,128]{3,0,2,1:T(8,128)S(1)} %get-tuple-element.12), channel_id=1, source_target_pairs={{0,4},{4,8},{8,12},{12,16},{16,20},{20,24},{24,28},{1,5},{5,9},{9,... | collective-permute-start | bytes 589832 | tf_op jit(solution)/shard_map/ppermute | solution.py:23
  128.8 6.6 %collective-permute-start.20 = (f32[64,1,8,128]{3,0,2,1:T(8,128)S(1)}, f32[64,1,8,128]{3,0,2,1:T(8,128)S(1)}, u32[]{:S(2)}, u32[]{:S(2)}) collective-permute-start(f32[64,1,8,128]{3,0,2,1:T(8,128)S(1)} %get-tuple-element.27), channel_id=1, source_target_pairs={{32,0},{64,32},{96,64},{128,96},{160,128},{192,160},{224,192},{33,... | collective-permute-start | bytes 786440 | tf_op jit(solution)/shard_map/ppermute | solution.py:26
  130.1 6.4 %collective-permute-start.21 = (f32[64,1,8,128]{3,0,2,1:T(8,128)S(1)}, f32[64,1,8,128]{3,0,2,1:T(8,128)S(1)}, u32[]{:S(2)}, u32[]{:S(2)}) collective-permute-start(f32[64,1,8,128]{3,0,2,1:T(8,128)S(1)} %get-tuple-element.26), channel_id=1, source_target_pairs={{0,32},{32,64},{64,96},{96,128},{128,160},{160,192},{192,224},{1,3... | collective-permute-start | bytes 786440 | tf_op jit(solution)/shard_map/ppermute | solution.py:23
  136.6 7.6 %collective-permute-start.22 = (f32[64,6,1,128]{3,0,2,1:T(8,128)S(1)}, f32[64,6,1,128]{3,0,2,1:T(8,128)S(1)}, u32[]{:S(2)}, u32[]{:S(2)}) collective-permute-start(f32[64,6,1,128]{3,0,2,1:T(8,128)S(1)} %get-tuple-element.11), channel_id=1, source_target_pairs={{4,0},{8,4},{12,8},{16,12},{20,16},{24,20},{28,24},{5,1},{9,5},{13... | collective-permute-start | bytes 589832 | tf_op jit(solution)/shard_map/ppermute | solution.py:26
  138.5 10.4 %collective-permute-start.23 = (f32[64,6,1,128]{3,0,2,1:T(8,128)S(1)}, f32[64,6,1,128]{3,0,2,1:T(8,128)S(1)}, u32[]{:S(2)}, u32[]{:S(2)}) collective-permute-start(f32[64,6,1,128]{3,0,2,1:T(8,128)S(1)} %get-tuple-element.10), channel_id=1, source_target_pairs={{0,4},{4,8},{8,12},{12,16},{16,20},{20,24},{24,28},{1,5},{5,9},{9,... | collective-permute-start | bytes 589832 | tf_op jit(solution)/shard_map/ppermute | solution.py:23
  152.7 6.6 %collective-permute-start.24 = (f32[64,1,8,128]{3,0,2,1:T(8,128)S(1)}, f32[64,1,8,128]{3,0,2,1:T(8,128)S(1)}, u32[]{:S(2)}, u32[]{:S(2)}) collective-permute-start(f32[64,1,8,128]{3,0,2,1:T(8,128)S(1)} %get-tuple-element.25), channel_id=1, source_target_pairs={{32,0},{64,32},{96,64},{128,96},{160,128},{192,160},{224,192},{33,... | collective-permute-start | bytes 786440 | tf_op jit(solution)/shard_map/ppermute | solution.py:26
  154.0 6.4 %collective-permute-start.25 = (f32[64,1,8,128]{3,0,2,1:T(8,128)S(1)}, f32[64,1,8,128]{3,0,2,1:T(8,128)S(1)}, u32[]{:S(2)}, u32[]{:S(2)}) collective-permute-start(f32[64,1,8,128]{3,0,2,1:T(8,128)S(1)} %get-tuple-element.24), channel_id=1, source_target_pairs={{0,32},{32,64},{64,96},{96,128},{128,160},{160,192},{192,224},{1,3... | collective-permute-start | bytes 786440 | tf_op jit(solution)/shard_map/ppermute | solution.py:23
  160.4 7.6 %collective-permute-start.26 = (f32[64,6,1,128]{3,0,2,1:T(8,128)S(1)}, f32[64,6,1,128]{3,0,2,1:T(8,128)S(1)}, u32[]{:S(2)}, u32[]{:S(2)}) collective-permute-start(f32[64,6,1,128]{3,0,2,1:T(8,128)S(1)} %get-tuple-element.9), channel_id=1, source_target_pairs={{4,0},{8,4},{12,8},{16,12},{20,16},{24,20},{28,24},{5,1},{9,5},{13... | collective-permute-start | bytes 589832 | tf_op jit(solution)/shard_map/ppermute | solution.py:26
  162.3 10.4 %collective-permute-start.27 = (f32[64,6,1,128]{3,0,2,1:T(8,128)S(1)}, f32[64,6,1,128]{3,0,2,1:T(8,128)S(1)}, u32[]{:S(2)}, u32[]{:S(2)}) collective-permute-start(f32[64,6,1,128]{3,0,2,1:T(8,128)S(1)} %get-tuple-element.8), channel_id=1, source_target_pairs={{0,4},{4,8},{8,12},{12,16},{16,20},{20,24},{24,28},{1,5},{5,9},{9,... | collective-permute-start | bytes 589832 | tf_op jit(solution)/shard_map/ppermute | solution.py:23
  176.1 6.6 %collective-permute-start.28 = (f32[64,1,8,128]{3,0,2,1:T(8,128)S(1)}, f32[64,1,8,128]{3,0,2,1:T(8,128)S(1)}, u32[]{:S(2)}, u32[]{:S(2)}) collective-permute-start(f32[64,1,8,128]{3,0,2,1:T(8,128)S(1)} %get-tuple-element.23), channel_id=1, source_target_pairs={{32,0},{64,32},{96,64},{128,96},{160,128},{192,160},{224,192},{33,... | collective-permute-start | bytes 786440 | tf_op jit(solution)/shard_map/ppermute | solution.py:26
  177.4 6.4 %collective-permute-start.29 = (f32[64,1,8,128]{3,0,2,1:T(8,128)S(1)}, f32[64,1,8,128]{3,0,2,1:T(8,128)S(1)}, u32[]{:S(2)}, u32[]{:S(2)}) collective-permute-start(f32[64,1,8,128]{3,0,2,1:T(8,128)S(1)} %get-tuple-element.22), channel_id=1, source_target_pairs={{0,32},{32,64},{64,96},{96,128},{128,160},{160,192},{192,224},{1,3... | collective-permute-start | bytes 786440 | tf_op jit(solution)/shard_map/ppermute | solution.py:23
  183.9 7.6 %collective-permute-start.30 = (f32[64,6,1,128]{3,0,2,1:T(8,128)S(1)}, f32[64,6,1,128]{3,0,2,1:T(8,128)S(1)}, u32[]{:S(2)}, u32[]{:S(2)}) collective-permute-start(f32[64,6,1,128]{3,0,2,1:T(8,128)S(1)} %get-tuple-element.7), channel_id=1, source_target_pairs={{4,0},{8,4},{12,8},{16,12},{20,16},{24,20},{28,24},{5,1},{9,5},{13... | collective-permute-start | bytes 589832 | tf_op jit(solution)/shard_map/ppermute | solution.py:26
  185.8 10.4 %collective-permute-start.31 = (f32[64,6,1,128]{3,0,2,1:T(8,128)S(1)}, f32[64,6,1,128]{3,0,2,1:T(8,128)S(1)}, u32[]{:S(2)}, u32[]{:S(2)}) collective-permute-start(f32[64,6,1,128]{3,0,2,1:T(8,128)S(1)} %get-tuple-element.6), channel_id=1, source_target_pairs={{0,4},{4,8},{8,12},{12,16},{16,20},{20,24},{24,28},{1,5},{5,9},{9,... | collective-permute-start | bytes 589832 | tf_op jit(solution)/shard_map/ppermute | solution.py:23
  199.7 66.2 %copy-start.4 = (s32[256]{0:T(256)S(1)}, s32[256]{0:T(256)}, u32[]{:S(2)}) copy-start(s32[256]{0:T(256)} %param.16) | copy-start | bytes 3076
  201.1 224.2 %all-gather.6.cloned.1.call-start = ((), (), s32[]{:S(2)}) async-start(), calls=%async_computation.1 | async-start | bytes 4259840 | tf_op jit(solution)/shard_map/all_gather | solution.py:13
  262.7 3.9 copy-start.2
Sparse Core Ops, SparseCore 0:
  201.2 61.4 all-gather.3
  266.0 159.1 all-gather.5
